TPU v7x, 256 devices: a whole 4x4x8 slice. The times are simulated.
256 devices in a mesh: gx: 8 (over x, core), gy: 8 (over z), gz: 4 (over y).
Axes of the slice: x: 4, y: 4, z: 8, core: 2. Of those that a mesh axis runs over, the one named last changes fastest.
Arguments:
- vec_prev: float32 [2, 1024, 128, 512], P(None, 'gx', 'gy', 'gz'), may hold values from -4 to 4
- source: float32 [2, 1024, 128, 512], P(None, 'gx', 'gy', 'gz'), may hold values from -6 to 6
- mag_mat: int32 [1024, 128, 512], P('gx', 'gy', 'gz'), may hold values from 0 to 3
- send_idx: int32 [256, 64, 128], P(('gx', 'gy', 'gz')), may hold values from 0 to 262143
- send_count: int32 [256, 64], P(('gx', 'gy', 'gz')), may hold values from 1 to 128, as said below
- recv_cell: int32 [256, 64, 128], P(('gx', 'gy', 'gz')), may hold values from 0 to 131071
- temp: float32 [256, 128, 1024], P('gx', 'gy', 'gz'), may hold values from 0 to 2
- heat_mat: int32 [256, 128, 1024], P('gx', 'gy', 'gz'), may hold values from 0 to 3
Outputs:
- potential: float32 [2, 1024, 128, 512], P(None, 'gx', 'gy', 'gz')
- temp_out: float32 [256, 128, 1024], P('gx', 'gy', 'gz')
Inputs may be any that keep to these rules, and one draw needn't show every extreme that they name: `send_count`: in every draw one peer position receives 128 from every device.
All inputs are finite; a program needn't handle non-finite values.
Results may differ from a plain program's by a relative error of at most 0.00002.
Values sent between devices are 32-bit elements; how exact they have to be, the bound alone decides.
A program may use at most 128 MiB of HBM per device.

v0:
```python
import jax
import jax.numpy as jnp
from jax import lax
from jax.experimental import pallas as pl
from jax.experimental.pallas import tpu as pltpu
from jax.sharding import PartitionSpec as P

sigma_table = (0.0, 3.0, 1.5, 6.0)
conduct_table = (1.0, 0.15, 0.05, 0.9)
capacity_table = (7.0, 2.0, 1.0, 6.0)
upwind_rate = 0.3
real_table = tuple(6.0 / (36.0 + s * s) for s in sigma_table)
imag_table = tuple(s / (36.0 + s * s) for s in sigma_table)
inverse_capacity = tuple(1.0 / c for c in capacity_table)

MESH = pl.DeviceIdType.MESH
LANES = 128
AXES = ("gx", "gy", "gz")
f32 = jnp.float32
bf16 = jnp.bfloat16


def lookup(material, table):
    first = jnp.where(material == 0, f32(table[0]), f32(table[1]))
    second = jnp.where(material == 2, f32(table[2]), f32(table[3]))
    return jnp.where(material < 2, first, second)


def halves(value):
    high = value.astype(bf16)
    return high, (value - high.astype(f32)).astype(bf16)


class Exchange:
    def __init__(self, number, sends, receives, faces):
        self.number, self.sends, self.receives, self.faces = number, sends, receives, faces

    def each(self):
        for at, (axis, (low_face, high_face), (low_halo, high_halo)) in enumerate(self.faces):
            me, count = lax.axis_index(axis), lax.axis_size(axis)
            up = pltpu.make_async_remote_copy(
                src_ref=high_face, dst_ref=low_halo,
                send_sem=self.sends.at[self.number, 2 * at],
                recv_sem=self.receives.at[self.number, 2 * at],
                device_id={axis: wrap(me + 1, count)}, device_id_type=MESH,
            )
            down = pltpu.make_async_remote_copy(
                src_ref=low_face, dst_ref=high_halo,
                send_sem=self.sends.at[self.number, 2 * at + 1],
                recv_sem=self.receives.at[self.number, 2 * at + 1],
                device_id={axis: wrap(me + count - 1, count)}, device_id_type=MESH,
            )
            yield me > 0, me < count - 1, up, down, low_halo, high_halo

    def start(self, only=AXES):
        for (axis, _, _), (below, above, up, down, _, _) in zip(self.faces, self.each()):
            if axis in only:
                pl.when(above)(up.start)
                pl.when(below)(down.start)

    def wait(self):
        for below, above, up, down, low_halo, high_halo in self.each():
            pl.when(below)(up.wait_recv)
            pl.when(above)(down.wait_recv)

    def clear(self):
        for axis, _, (low_halo, high_halo) in self.faces:
            me, count = lax.axis_index(axis), lax.axis_size(axis)

            @pl.when(me == 0)
            def _():
                low_halo[...] = jnp.zeros(low_halo.shape, f32)

            @pl.when(me == count - 1)
            def _():
                high_halo[...] = jnp.zeros(high_halo.shape, f32)

    def drain(self):
        for below, above, up, down, _, _ in self.each():
            pl.when(above)(up.wait_send)
            pl.when(below)(down.wait_send)


def iota(shape, dim):
    return lax.broadcasted_iota(jnp.int32, shape, dim)


def wrap(value, count):
    return value & (count - 1) if count & (count - 1) == 0 else lax.rem(value, count)


def face_columns(planes):
    stacked = jnp.concatenate(planes, axis=0)
    depth = stacked.shape[1]
    low = jnp.transpose(stacked[:, :LANES])
    high = low if depth == LANES else jnp.transpose(stacked[:, depth - LANES:])
    return low[0:1, :], high[LANES - 1:LANES, :]


def halo_columns(low, high):
    sub = iota((LANES, LANES), 0)
    return jnp.transpose(jnp.where(sub == 0, low, jnp.where(sub == LANES - 1, high, f32(0.0))))


def column_shifts(plane, halo):
    rows, depth = plane.shape
    lane = iota((rows, depth), 1)
    if depth > LANES and halo.ndim:
        halo = jnp.concatenate([halo] * (depth // LANES), axis=1)
    return (
        jnp.where(lane == 0, halo, pltpu.roll(plane, 1, 1)),
        jnp.where(lane == depth - 1, halo, pltpu.roll(plane, depth - 1, 1)),
    )


def row_shifts(plane, low, high):
    rows, depth = plane.shape
    row = iota((rows, depth), 0)
    return (
        jnp.where(row == 0, low, pltpu.roll(plane, 1, 0)),
        jnp.where(row == rows - 1, high, pltpu.roll(plane, rows - 1, 0)),
    )


def kernel(
    vec_hbm, source_hbm, mag_hbm, idx_hbm, count_hbm, cell_hbm, temp_hbm, heat_hbm,
    potential_hbm, out_hbm,
    field0, field1, source, mag, idx, count_ref, cell, temp0, temp1, temp2, heat_mat, kcell, coef, rate,
    near, xh_m, ys_m, yh_m, zs_m, zh_m, xh_t, partial, ys_t, yh_t, zs_t, zh_t,
    table, chosen, sent, landed, one_hot, v_high, v_low, heat,
    load_sems, halo_send, halo_recv, slot_send, slot_recv,
):
    _, size_x, size_y, size_z = source.shape
    heat_x, heat_y, heat_z = heat_mat.shape
    n_gx, n_gy = lax.axis_size("gx"), lax.axis_size("gy")
    ix, iy, iz, n_gz = lax.axis_index("gx"), lax.axis_index("gy"), lax.axis_index("gz"), lax.axis_size("gz")
    group, here = n_gx * n_gy, ix * n_gy + iy

    loads = [
        pltpu.make_async_copy(src, dst, load_sems.at[at])
        for at, (src, dst) in enumerate(
            [
                (vec_hbm, field0.at[:, pl.ds(1, size_x)]),
                (temp_hbm, temp0.at[pl.ds(1, heat_x)]),
                (heat_hbm, heat_mat),
                (mag_hbm, mag),
                (source_hbm, source),
                (idx_hbm.at[0], idx),
                (cell_hbm.at[0], cell),
                (count_hbm, count_ref),
            ]
        )
    ]
    for load in loads:
        load.start()

    barrier = pltpu.get_barrier_semaphore()

    def greet(device):
        pl.semaphore_signal(barrier, inc=1, device_id=device, device_id_type=MESH)

    for step in range(1, n_gy):
        greet({"gy": wrap(iy + step, n_gy)})

    @pl.loop(1, n_gx)
    def _(step):
        for other in range(n_gy):
            greet({"gx": wrap(ix + step, n_gx), "gy": other})

    @pl.when(iz > 0)
    def _():
        greet({"gz": wrap(iz + n_gz - 1, n_gz)})

    @pl.when(iz < n_gz - 1)
    def _():
        greet({"gz": wrap(iz + 1, n_gz)})

    def faces(x_low, x_high, x_low_halo, x_high_halo, ys, yh, zs, zh, at):
        return [
            ("gx", (x_low, x_high), (x_low_halo, x_high_halo)),
            ("gy", (ys.at[at, 0], ys.at[at, 1]), (yh.at[at, 0], yh.at[at, 1])),
            ("gz", (zs.at[at, 0], zs.at[at, 1]), (zh.at[at, 0], zh.at[at, 1])),
        ]

    def mag_round(number, field):
        return Exchange(
            number, halo_send, halo_recv,
            faces(
                field.at[:, 1], field.at[:, size_x], xh_m.at[number, 0], xh_m.at[number, 1],
                ys_m, yh_m, zs_m, zh_m, number,
            ),
        )

    def heat_round(number, at, state):
        return Exchange(
            number, halo_send, halo_recv,
            faces(
                state.at[1], state.at[heat_x], xh_t.at[at, 0], xh_t.at[at, 1],
                ys_t, yh_t, zs_t, zh_t, at,
            ),
        )

    round0 = mag_round(0, field0)
    round1 = mag_round(1, field1)
    round_t = heat_round(2, 0, temp0)
    round_k = heat_round(3, 1, kcell)
    round_1 = heat_round(4, 2, temp1)
    round_2 = heat_round(5, 3, temp2)
    rounds = (round0, round1, round_t, round_k, round_1, round_2)
    for each in rounds:
        each.clear()
    for field in (field0, field1):
        for x in (0, size_x + 1):
            field[:, x] = jnp.zeros((2, size_y, size_z), f32)
    for state in (temp1, temp2):
        for x in (0, heat_x + 1):
            state[x] = jnp.zeros((heat_y, heat_z), f32)

    block = LANES // size_y
    block_t = LANES // heat_y

    def pack_mag(at, j, part, planes):
        for i, plane in enumerate(planes):
            ys_m[at, 0, part, j * block + i] = plane[0:1, :]
            ys_m[at, 1, part, j * block + i] = plane[size_y - 1:size_y, :]
        zs_m[at, 0, part, j], zs_m[at, 1, part, j] = face_columns(planes)

    def pack_heat(at, j, planes):
        for i, plane in enumerate(planes):
            ys_t[at, 0, j * block_t + i] = plane[0:1, :]
            ys_t[at, 1, j * block_t + i] = plane[heat_y - 1:heat_y, :]

    def send_heat(each, at, state):
        each.start(("gx", "gy"))

        @pl.loop(0, heat_x // block_t)
        def _(j):
            planes = [state[j * block_t + i + 1] for i in range(block_t)]
            zs_t[at, 0, j], zs_t[at, 1, j] = face_columns(planes)

        each.start(("gz",))

    loads[0].wait()

    @pl.loop(0, size_x // block)
    def _(j):
        for part in range(2):
            pack_mag(0, j, part, [field0[part, j * block + i + 1] for i in range(block)])

    pl.semaphore_wait(barrier, group - 1 + (iz > 0).astype(jnp.int32) + (iz < n_gz - 1).astype(jnp.int32))
    round0.start()

    loads[1].wait()
    loads[2].wait()

    @pl.loop(0, heat_x // block_t)
    def _(j):
        planes = []
        for i in range(block_t):
            x = j * block_t + i
            planes.append(lookup(heat_mat[x], conduct_table))
            kcell[x + 1] = planes[-1]
        pack_heat(1, j, planes)
        pack_heat(0, j, [temp0[j * block_t + i + 1] for i in range(block_t)])

    send_heat(round_t, 0, temp0)
    send_heat(round_k, 1, kcell)

    def add_near(field):
        @pl.loop(0, size_x // block)
        def _(j):
            for part in range(2):
                for i in range(block):
                    x = j * block + i
                    plane = field[part, x + 1]
                    low_y, high_y = row_shifts(plane, f32(0.0), f32(0.0))
                    low_z, high_z = column_shifts(plane, f32(0.0))
                    near[part, x] = (field[part, x] + field[part, x + 2]) + (low_y + high_y) + (low_z + high_z)

    add_near(field0)
    for load in loads[3:]:
        load.wait()

    row_m = iota((size_y, size_z), 0)

    def add_planes(at):
        for part in range(2):
            near[part, 0] += xh_m[at, 0, part]
            near[part, size_x - 1] += xh_m[at, 1, part]

    def relaxed(at, j):
        columns = [halo_columns(zh_m[at, 0, part, j], zh_m[at, 1, part, j]) for part in range(2)]
        result = ([], [])
        for i in range(block):
            x = j * block + i
            total = []
            for part in range(2):
                rows = jnp.where(
                    row_m == 0, yh_m[at, 0, part, x], jnp.where(row_m == size_y - 1, yh_m[at, 1, part, x], f32(0.0))
                )
                total.append(
                    (source[part, x] + near[part, x]) + (rows + columns[part][i * size_y:(i + 1) * size_y, :])
                )
            material = mag[x]
            real, imag = lookup(material, real_table), lookup(material, imag_table)
            result[0].append(real * total[0] + imag * total[1])
            result[1].append(real * total[1] - imag * total[0])
        return result

    round0.wait()
    add_planes(0)

    @pl.loop(0, size_x // block)
    def _(j):
        for part, planes in enumerate(relaxed(0, j)):
            for i, plane in enumerate(planes):
                field1[part, j * block + i + 1] = plane
            pack_mag(1, j, part, planes)

    round1.start()

    round_t.wait()
    round_k.wait()
    for at, state in enumerate((temp0, kcell)):
        state[0] = xh_t[at, 0]
        state[heat_x + 1] = xh_t[at, 1]

    def neighbours(at, state, j):
        columns = halo_columns(zh_t[at, 0, j], zh_t[at, 1, j])
        for i in range(block_t):
            x = j * block_t + i
            plane = state[x + 1]
            low_y, high_y = row_shifts(plane, yh_t[at, 0, x], yh_t[at, 1, x])
            low_z, high_z = column_shifts(plane, columns[i * heat_y:(i + 1) * heat_y, :])
            yield x, plane, (state[x], state[x + 2], low_y, high_y, low_z, high_z)

    @pl.loop(0, heat_x // block_t)
    def _(j):
        for (x, conduct, beside), (_, plane, around) in zip(neighbours(1, kcell, j), neighbours(0, temp0, j)):
            material = heat_mat[x]
            inverse = lookup(material, inverse_capacity)
            upwind = jnp.where(material == 1, f32(upwind_rate), f32(0.0))
            twice = (2.0 * inverse) * conduct
            centre = 1.0 - upwind
            total = jnp.zeros(plane.shape, f32)
            for side in range(6):
                weight = twice * beside[side] / (conduct + beside[side])
                centre = centre - weight
                if side == 4:
                    weight = weight + upwind
                coef[side, x] = weight
                total = total + weight * around[side]
            coef[6, x] = centre
            rate[x] = inverse
            temp1[x + 1] = total + centre * plane

    add_near(field1)
    round1.wait()
    add_planes(1)
    round0.drain()

    @pl.loop(0, size_x // block)
    def _(j):
        losses = []
        for i, planes in enumerate(zip(*relaxed(1, j))):
            x = j * block + i
            field0[0, x + 1] = planes[0]
            field0[1, x + 1] = planes[1]
            losses.append(
                (0.5 * lookup(mag[x], sigma_table)) * (planes[0] * planes[0] + planes[1] * planes[1])
            )
        high, low = halves(jnp.transpose(jnp.concatenate(losses, axis=0)))
        at = pl.ds(pl.multiple_of(j * LANES, LANES), LANES)
        table[0:size_z, at] = high
        table[size_z:2 * size_z, at] = low

    store_potential = pltpu.make_async_copy(
        field0.at[:, pl.ds(1, size_x)], potential_hbm, load_sems.at[8]
    )
    store_potential.start()

    table_rows = size_x * size_y
    width = n_gy * LANES
    slot = iota((1, LANES), 1)
    row16 = lax.broadcasted_iota(jnp.int16, (table_rows, LANES), 0)
    sub_z = iota((size_z, LANES), 0)

    def slot_copy(gx, gy):
        return pltpu.make_async_remote_copy(
            src_ref=sent.at[gx * n_gy + gy], dst_ref=landed.at[here],
            send_sem=slot_send, recv_sem=slot_recv.at[ix],
            device_id={"gx": gx, "gy": gy}, device_id_type=MESH,
        )

    def slots_from(gx, count):
        rows = landed.at[pl.ds(gx * n_gy, count)]
        return pltpu.make_async_remote_copy(
            src_ref=rows, dst_ref=rows, send_sem=slot_send, recv_sem=slot_recv.at[gx],
            device_id={"gx": wrap(ix + 1, n_gx)}, device_id_type=MESH,
        )

    @pl.loop(0, n_gx)
    def _(step):
        target = wrap(ix + step + 1, n_gx)
        first = target * n_gy
        cells = []
        for p in range(n_gy):
            wanted = jnp.where(slot < count_ref[0, first + p], idx[pl.ds(first + p, 1), :], -1)
            cells.append(wanted)
            row = jnp.broadcast_to(lax.shift_right_arithmetic(wanted, 7).astype(jnp.int16), (table_rows, LANES))
            chosen[:, LANES * p:LANES * (p + 1)] = jnp.where(row16 == row, jnp.ones((), bf16), jnp.zeros((), bf16))
        found = jnp.dot(table[...], chosen[...], preferred_element_type=f32)
        found = found[:size_z] + found[size_z:]
        for p in range(n_gy):
            hit = sub_z == (cells[p] & (size_z - 1))
            sent[first + p] = jnp.sum(
                jnp.where(hit, found[:, LANES * p:LANES * (p + 1)], 0.0), axis=0, keepdims=True
            )
        for p in range(n_gy):
            @pl.when(first + p != here)
            def _():
                slot_copy(target, p).start()

    landed[here] = sent[here]

    row_h = lax.broadcasted_iota(jnp.int16, (heat_x * heat_y, LANES), 0)
    row_z = lax.broadcasted_iota(jnp.int16, (heat_z, LANES), 0)
    shift = heat_z.bit_length() - 1
    heat[...] = jnp.zeros(heat.shape, f32)
    per = one_hot.shape[1] // LANES // n_gy
    zero16 = jnp.zeros((), bf16)
    transposed = (((1,), (1,)), ((), ()))

    @pl.loop(0, n_gx // per)
    def _(step):
        peers = []
        for k in range(per):
            gx = wrap(ix + 2 * n_gx - 1 - (step * per + k), n_gx)

            @pl.when(gx != ix)
            def _():
                slots_from(gx, n_gy).wait_recv()

            @pl.when(gx == ix)
            def _():
                slots_from(gx, n_gy - 1).wait_recv()

            peers += [gx * n_gy + gy for gy in range(n_gy)]

        for p, peer in enumerate(peers):
            target = cell[pl.ds(peer, 1), :]
            high, low = halves(landed[peer])
            at = slice(LANES * p, LANES * (p + 1))
            row = jnp.broadcast_to(lax.shift_right_logical(target, shift).astype(jnp.int16), row_h.shape)
            one_hot[:, at] = jnp.where(row_h == row, jnp.ones((), bf16), zero16)
            hit = row_z == jnp.broadcast_to((target & (heat_z - 1)).astype(jnp.int16), row_z.shape)
            v_high[:, at] = jnp.where(hit, jnp.broadcast_to(high, row_z.shape), zero16)
            v_low[:, at] = jnp.where(hit, jnp.broadcast_to(low, row_z.shape), zero16)
        heat[...] += lax.dot_general(
            one_hot[...], v_high[...], transposed, preferred_element_type=f32
        ) + lax.dot_general(one_hot[...], v_low[...], transposed, preferred_element_type=f32)

    @pl.loop(0, heat_x // block_t)
    def _(j):
        planes = []
        for i in range(block_t):
            x = j * block_t + i
            gain = heat[pl.ds(pl.multiple_of(x * heat_y, heat_y), heat_y), :] * rate[x]
            rate[x] = gain
            planes.append(temp1[x + 1] + gain)
            temp1[x + 1] = planes[-1]
        pack_heat(2, j, planes)

    send_heat(round_1, 2, temp1)

    row_t = iota((heat_y, heat_z), 0)
    depth_t = iota((heat_y, heat_z), 1)

    def step_near(state):
        @pl.loop(0, heat_x // block_t)
        def _(j):
            for i in range(block_t):
                x = j * block_t + i
                plane = state[x + 1]
                around = (
                    (state[x], state[x + 2])
                    + row_shifts(plane, f32(0.0), f32(0.0))
                    + column_shifts(plane, f32(0.0))
                )
                total = coef[6, x] * plane + rate[x]
                for side, other in enumerate(around):
                    total = total + coef[side, x] * other
                partial[x] = total

    def add_ends(at):
        partial[0] += coef[0, 0] * xh_t[at, 0]
        partial[heat_x - 1] += coef[1, heat_x - 1] * xh_t[at, 1]

    def stepped(at, j):
        columns = halo_columns(zh_t[at, 0, j], zh_t[at, 1, j])
        columns = jnp.concatenate([columns] * (heat_z // LANES), axis=1)
        for i in range(block_t):
            x = j * block_t + i
            column = columns[i * heat_y:(i + 1) * heat_y, :]
            low_y, high_y = coef[2, x] * yh_t[at, 0, x], coef[3, x] * yh_t[at, 1, x]
            low_z, high_z = coef[4, x] * column, coef[5, x] * column
            zero = f32(0.0)
            rows = jnp.where(row_t == 0, low_y, jnp.where(row_t == heat_y - 1, high_y, zero))
            ends = jnp.where(depth_t == 0, low_z, jnp.where(depth_t == heat_z - 1, high_z, zero))
            yield x, partial[x] + (rows + ends)

    step_near(temp1)
    for each in (round1, round_t, round_k):
        each.drain()
    everyone = sent.at[pl.ds(0, group - 1)]
    pltpu.make_async_remote_copy(
        src_ref=everyone, dst_ref=everyone, send_sem=slot_send, recv_sem=slot_recv.at[0],
        device_id={"gx": wrap(ix + 1, n_gx)}, device_id_type=MESH,
    ).wait_send()
    store_potential.wait()
    round_1.wait()
    add_ends(2)

    @pl.loop(0, heat_x // block_t)
    def _(j):
        planes = []
        for x, plane in stepped(2, j):
            temp2[x + 1] = plane
            planes.append(plane)
        pack_heat(3, j, planes)

    send_heat(round_2, 3, temp2)
    step_near(temp2)
    round_1.drain()
    round_2.wait()
    add_ends(3)

    @pl.loop(0, heat_x // block_t)
    def _(j):
        for x, plane in stepped(3, j):
            temp0[x + 1] = plane

    store_temp = pltpu.make_async_copy(temp0.at[pl.ds(1, heat_x)], out_hbm, load_sems.at[9])
    store_temp.start()
    round_2.drain()

    store_temp.wait()


def finish(potential_in, temp_in, potential_out, temp_out, potential, temp, sems):
    pieces = 4
    size_x = potential.shape[1] // pieces
    steps = []
    for piece in range(pieces):
        at = pl.ds(piece * size_x, size_x)
        steps.append((potential_in.at[:, at], potential.at[:, at], potential_out.at[:, at]))
    steps.append((temp_in, temp, temp_out))
    arrive = [pltpu.make_async_copy(a, b, sems.at[0, k]) for k, (a, b, _) in enumerate(steps)]
    leave = [pltpu.make_async_copy(b, c, sems.at[1, k]) for k, (_, b, c) in enumerate(steps)]
    for copy in arrive:
        copy.start()
    for copy, out in zip(arrive, leave):
        copy.wait()
        out.start()
    for out in leave:
        out.wait()


def shards(vec_prev, source, mag_mat, send_idx, send_count, recv_cell, temp, heat_mat):
    _, size_x, size_y, size_z = vec_prev.shape
    heat_x, heat_y, heat_z = temp.shape
    n_gx, n_gy = lax.axis_size("gx"), lax.axis_size("gy")
    group = n_gx * n_gy
    per = min(2, n_gx) * n_gy
    vmem = pltpu.VMEM
    anywhere = pl.BlockSpec(memory_space=pl.ANY)
    results = pl.pallas_call(
        kernel,
        out_shape=(
            jax.ShapeDtypeStruct(vec_prev.shape, f32),
            jax.ShapeDtypeStruct(temp.shape, f32),
        ),
        in_specs=[anywhere] * 8,
        out_specs=(anywhere, anywhere),
        scratch_shapes=[
            vmem((2, size_x + 2, size_y, size_z), f32),
            vmem((2, size_x + 2, size_y, size_z), f32),
            vmem(source.shape, f32),
            vmem(mag_mat.shape, jnp.int32),
            vmem(send_idx.shape[1:], jnp.int32),
            pltpu.SMEM(send_count.shape, jnp.int32),
            vmem(recv_cell.shape[1:], jnp.int32),
            vmem((heat_x + 2, heat_y, heat_z), f32),
            vmem((heat_x + 2, heat_y, heat_z), f32),
            vmem((heat_x + 2, heat_y, heat_z), f32),
            vmem(heat_mat.shape, jnp.int32),
            vmem((heat_x + 2, heat_y, heat_z), f32),
            vmem((7, heat_x, heat_y, heat_z), f32),
            vmem((heat_x, heat_y, heat_z), f32),
            vmem(source.shape, f32),
            vmem((2, 2, 2, size_y, size_z), f32),
            vmem((2, 2, 2, size_x, 1, size_z), f32),
            vmem((2, 2, 2, size_x, 1, size_z), f32),
            vmem((2, 2, 2, size_x * size_y // LANES, 1, LANES), f32),
            vmem((2, 2, 2, size_x * size_y // LANES, 1, LANES), f32),
            vmem((4, 2, heat_y, heat_z), f32),
            vmem((heat_x, heat_y, heat_z), f32),
            vmem((4, 2, heat_x, 1, heat_z), f32),
            vmem((4, 2, heat_x, 1, heat_z), f32),
            vmem((4, 2, heat_x * heat_y // LANES, 1, LANES), f32),
            vmem((4, 2, heat_x * heat_y // LANES, 1, LANES), f32),
            vmem((2 * size_z, size_x * size_y), bf16),
            vmem((size_x * size_y, n_gy * LANES), bf16),
            vmem((group, 1, LANES), f32),
            vmem((group, 1, LANES), f32),
            vmem((heat_x * heat_y, per * LANES), bf16),
            vmem((heat_z, per * LANES), bf16),
            vmem((heat_z, per * LANES), bf16),
            vmem((heat_x * heat_y, heat_z), f32),
            pltpu.SemaphoreType.DMA((10,)),
            pltpu.SemaphoreType.DMA((6, 6)),
            pltpu.SemaphoreType.DMA((6, 6)),
            pltpu.SemaphoreType.DMA,
            pltpu.SemaphoreType.DMA((n_gx,)),
        ],
        compiler_params=pltpu.CompilerParams(
            collective_id=0, has_side_effects=True, vmem_limit_bytes=60 << 20
        ),
    )(vec_prev, source, mag_mat, send_idx, send_count, recv_cell, temp, heat_mat)
    return pl.pallas_call(
        finish,
        out_shape=tuple(jax.ShapeDtypeStruct(result.shape, f32) for result in results),
        in_specs=[anywhere] * 2,
        out_specs=(anywhere, anywhere),
        scratch_shapes=[
            vmem(vec_prev.shape, f32),
            vmem(temp.shape, f32),
            pltpu.SemaphoreType.DMA((2, 5)),
        ],
        compiler_params=pltpu.CompilerParams(vmem_limit_bytes=60 << 20),
    )(*results)


def solution(mesh):
    placed = (
        P(None, "gx", "gy", "gz"),
        P(None, "gx", "gy", "gz"),
        P("gx", "gy", "gz"),
        P(("gx", "gy", "gz"), None, None),
        P(("gx", "gy", "gz"), None),
        P(("gx", "gy", "gz"), None, None),
        P("gx", "gy", "gz"),
        P("gx", "gy", "gz"),
    )
    return jax.shard_map(
        shards,
        mesh=mesh,
        in_specs=placed,
        out_specs=(P(None, "gx", "gy", "gz"), P("gx", "gy", "gz")),
        check_vma=False,
    )
```

profile of v0, /device:TPU:8, one launch (start us, length us, event | category | flops | bytes accessed | tf_op | source)
XLA Modules:
  0.0 55.7 jit_solution(16046854669882696024)
XLA Ops:
  0.6 52.5 %shard_map.95 = (f32[2,128,16,128]{3,2,1,0:T(8,128)}, f32[32,16,256]{2,1,0:T(8,128)}) custom-call(f32[2,128,16,128]{3,2,1,0:T(8,128)} %vec_hbm.1, f32[2,128,16,128]{3,2,1,0:T(8,128)} %source_hbm.1, s32[128,16,128]{2,1,0:T(8,128)} %mag_hbm.1, s32[1,64,128]{2,1,0:T(8,128)} %idx_hbm.1, s32[1,64]{1,0:T(1,128)} %count_hbm.1, s32[1,64,128]{2,1,0:T(8,128)} %cell_hbm.1, ...), custom_call_target="tpu_custom_call" | custom-call | tf_op jit(solution)/shard_map/pallas_call | solution.py:577
  53.1 2.6 %shard_map.96 = (f32[2,128,16,128]{3,2,1,0:T(8,128)}, f32[32,16,256]{2,1,0:T(8,128)}) custom-call(f32[2,128,16,128]{3,2,1,0:T(8,128)} %get-tuple-element.4.potential_in, f32[32,16,256]{2,1,0:T(8,128)} %get-tuple-element.5.temp_in), custom_call_target="tpu_custom_call" | custom-call | tf_op jit(solution)/shard_map/pallas_call | solution.py:630
where the time goes:
time: 55.8 us; the launch traced here: 55.7 us
  Pallas kernels  55.1 us (99%)
  between operations  0.64 us (1%)
    pallas_call x1, Pallas kernels, shards(): pl.pallas_call(kernel, out_shape=(jax.ShapeDtypeStruct(vec_prev.shape, f3...  52.5 us
    pallas_call x1, Pallas kernels, shards(): pl.pallas_call(finish, out_shape=tuple((jax.ShapeDtypeStruct(result.shape...  2.61 us

commit v1 on v0

--- a/solution.py
+++ b/solution.py
@@ -126,7 +126,7 @@
     vec_hbm, source_hbm, mag_hbm, idx_hbm, count_hbm, cell_hbm, temp_hbm, heat_hbm,
     potential_hbm, out_hbm,
     field0, field1, source, mag, idx, count_ref, cell, temp0, temp1, temp2, heat_mat, kcell, coef, rate,
-    near, xh_m, ys_m, yh_m, zs_m, zh_m, xh_t, partial, ys_t, yh_t, zs_t, zh_t,
+    near, xh_m, ys_m, yh_m, zs_m, zh_m, xs_t, xh_t, partial, ys_t, yh_t, zs_t, zh_t,
     table, chosen, sent, landed, one_hot, v_high, v_low, heat,
     load_sems, halo_send, halo_recv, slot_send, slot_recv,
 ):
@@ -202,11 +202,17 @@
 
     round0 = mag_round(0, field0)
     round1 = mag_round(1, field1)
-    round_t = heat_round(2, 0, temp0)
-    round_k = heat_round(3, 1, kcell)
+    both = pl.ds(0, 2)
+    round_t = Exchange(
+        2, halo_send, halo_recv,
+        faces(
+            xs_t.at[0], xs_t.at[1], xh_t.at[both, 0], xh_t.at[both, 1],
+            ys_t, yh_t, zs_t, zh_t, both,
+        ),
+    )
     round_1 = heat_round(4, 2, temp1)
     round_2 = heat_round(5, 3, temp2)
-    rounds = (round0, round1, round_t, round_k, round_1, round_2)
+    rounds = (round0, round1, round_t, round_1, round_2)
     for each in rounds:
         each.clear()
     for field in (field0, field1):
@@ -230,13 +236,14 @@
             ys_t[at, 0, j * block_t + i] = plane[0:1, :]
             ys_t[at, 1, j * block_t + i] = plane[heat_y - 1:heat_y, :]
 
-    def send_heat(each, at, state):
+    def send_heat(each, packed):
         each.start(("gx", "gy"))
 
         @pl.loop(0, heat_x // block_t)
         def _(j):
-            planes = [state[j * block_t + i + 1] for i in range(block_t)]
-            zs_t[at, 0, j], zs_t[at, 1, j] = face_columns(planes)
+            for at, state in packed:
+                planes = [state[j * block_t + i + 1] for i in range(block_t)]
+                zs_t[at, 0, j], zs_t[at, 1, j] = face_columns(planes)
 
         each.start(("gz",))
 
@@ -263,8 +270,10 @@
         pack_heat(1, j, planes)
         pack_heat(0, j, [temp0[j * block_t + i + 1] for i in range(block_t)])
 
-    send_heat(round_t, 0, temp0)
-    send_heat(round_k, 1, kcell)
+    for at, state in enumerate((temp0, kcell)):
+        xs_t[0, at] = state[1]
+        xs_t[1, at] = state[heat_x]
+    send_heat(round_t, ((0, temp0), (1, kcell)))
 
     def add_near(field):
         @pl.loop(0, size_x // block)
@@ -320,7 +329,6 @@
     round1.start()
 
     round_t.wait()
-    round_k.wait()
     for at, state in enumerate((temp0, kcell)):
         state[0] = xh_t[at, 0]
         state[heat_x + 1] = xh_t[at, 1]
@@ -471,7 +479,7 @@
             temp1[x + 1] = planes[-1]
         pack_heat(2, j, planes)
 
-    send_heat(round_1, 2, temp1)
+    send_heat(round_1, ((2, temp1),))
 
     row_t = iota((heat_y, heat_z), 0)
     depth_t = iota((heat_y, heat_z), 1)
@@ -510,7 +518,7 @@
             yield x, partial[x] + (rows + ends)
 
     step_near(temp1)
-    for each in (round1, round_t, round_k):
+    for each in (round1, round_t):
         each.drain()
     everyone = sent.at[pl.ds(0, group - 1)]
     pltpu.make_async_remote_copy(
@@ -529,7 +537,7 @@
             planes.append(plane)
         pack_heat(3, j, planes)
 
-    send_heat(round_2, 3, temp2)
+    send_heat(round_2, ((3, temp2),))
     step_near(temp2)
     round_1.drain()
     round_2.wait()
@@ -603,6 +611,7 @@
             vmem((2, 2, 2, size_x, 1, size_z), f32),
             vmem((2, 2, 2, size_x * size_y // LANES, 1, LANES), f32),
             vmem((2, 2, 2, size_x * size_y // LANES, 1, LANES), f32),
+            vmem((2, 2, heat_y, heat_z), f32),
             vmem((4, 2, heat_y, heat_z), f32),
             vmem((heat_x, heat_y, heat_z), f32),
             vmem((4, 2, heat_x, 1, heat_z), f32),

time: 55.8 us -> 55.8 us (level)
  no operation moved by 1% of the time
where the time goes in v1:
time: 55.8 us; the launch traced here: 55.7 us
  Pallas kernels  55.1 us (99%)
  between operations  0.64 us (1%)
    pallas_call x1, Pallas kernels, shards(): pl.pallas_call(kernel, out_shape=(jax.ShapeDtypeStruct(vec_prev.shape, f3...  52.5 us
    pallas_call x1, Pallas kernels, shards(): pl.pallas_call(finish, out_shape=tuple((jax.ShapeDtypeStruct(result.shape...  2.61 us

profile of v1, /device:TPU:8, one launch (start us, length us, event | category | flops | bytes accessed | tf_op | source)
XLA Modules:
  0.0 55.7 jit_solution(14907656228221757213)
XLA Ops:
  0.6 52.5 %shard_map.95 = (f32[2,128,16,128]{3,2,1,0:T(8,128)}, f32[32,16,256]{2,1,0:T(8,128)}) custom-call(f32[2,128,16,128]{3,2,1,0:T(8,128)} %vec_hbm.1, f32[2,128,16,128]{3,2,1,0:T(8,128)} %source_hbm.1, s32[128,16,128]{2,1,0:T(8,128)} %mag_hbm.1, s32[1,64,128]{2,1,0:T(8,128)} %idx_hbm.1, s32[1,64]{1,0:T(1,128)} %count_hbm.1, s32[1,64,128]{2,1,0:T(8,128)} %cell_hbm.1, ...), custom_call_target="tpu_custom_call" | custom-call | tf_op jit(solution)/shard_map/pallas_call | solution.py:585
  53.1 2.6 %shard_map.96 = (f32[2,128,16,128]{3,2,1,0:T(8,128)}, f32[32,16,256]{2,1,0:T(8,128)}) custom-call(f32[2,128,16,128]{3,2,1,0:T(8,128)} %get-tuple-element.4.potential_in, f32[32,16,256]{2,1,0:T(8,128)} %get-tuple-element.5.temp_in), custom_call_target="tpu_custom_call" | custom-call | tf_op jit(solution)/shard_map/pallas_call | solution.py:639
